TPU v7x, 512 devices: a whole 4x4x16 slice. The times are simulated.
512 devices in a mesh: ctx: 16 (over y, x_hi, core), cand: 32 (over z, x_lo).
Axes of the slice: x: 4 (x_hi: 2, x_lo: 2; x = x_hi * 2 + x_lo), y: 4, z: 16, core: 2. Of those that a mesh axis runs over, the one named last changes fastest.
Arguments:
- queries: bfloat16 [32, 128, 8192], P('cand', None, 'ctx'), may hold values from -4 to 4
- suffix_keys: bfloat16 [32, 128, 1024], P('cand'), may hold values from -10 to 10
- suffix_values: bfloat16 [32, 128, 1024], P('cand'), may hold values from -6 to 6
- prefix_keys: bfloat16 [16384, 1024], P('ctx'), may hold values from -9 to 9
- prefix_values: bfloat16 [16384, 1024], P('ctx'), may hold values from -6 to 6
- lengths: int32 [32], P('cand'), may hold values from 32 to 128, as said below
Outputs:
- attended: bfloat16 [32, 128, 8192], P('cand', None, 'ctx')
Inputs may be any that keep to these rules, and one draw needn't show every extreme that they name: `lengths`: one candidate has exactly 128 live tokens.
All inputs are finite; a program needn't handle non-finite values.
Results may differ from a plain program's by a relative error of at most 0.0055.
Values may be sent and summed in bfloat16 or wider, within the bound.
A program may use at most 64 MiB of HBM per device.

v0:
```python
import math

import jax
import jax.numpy as jnp
from jax import lax
from jax.sharding import PartitionSpec as P

H = 64
KVH = 8
HD = 128
LS = 128


def attend_prefix(gathered, prefix_keys, prefix_values):
    inv_root = 1.0 / math.sqrt(HD)
    cand_count = gathered.shape[0]
    groups = gathered.reshape(cand_count, LS, KVH, H // KVH, HD)
    key_rows = prefix_keys.reshape(-1, KVH, HD)
    value_rows = prefix_values.reshape(-1, KVH, HD)
    peaks, sums, partials = ([], [], [])
    for kv_head in range(KVH):
        scores = (
            jnp.einsum(
                "ctgd,pd->ctgp",
                groups[:, :, kv_head],
                key_rows[:, kv_head],
                preferred_element_type=jnp.float32,
            )
            * inv_root
        )
        peak = jnp.max(scores, axis=-1)
        weights = jnp.exp(scores - peak[..., None])
        block_sum = jnp.sum(weights, axis=-1)
        numerator = jnp.einsum(
            "ctgp,pd->ctgd",
            weights.astype(jnp.bfloat16),
            value_rows[:, kv_head],
            preferred_element_type=jnp.float32,
        )
        partials.append((numerator / block_sum[..., None]).astype(jnp.bfloat16))
        peaks.append(peak)
        sums.append(block_sum)
    peak_all = jnp.stack(peaks, axis=2).reshape(cand_count, LS, H)
    sum_all = jnp.stack(sums, axis=2).reshape(cand_count, LS, H)
    partial_all = jnp.stack(partials, axis=2).reshape(cand_count, LS, H, HD)
    return (peak_all, sum_all, partial_all)


def attend_suffix(own_queries, key_rows, value_rows, first_head):
    inv_root = 1.0 / math.sqrt(HD)
    cand_count = own_queries.shape[0]
    heads_here = own_queries.shape[2] // HD
    own = own_queries.reshape(cand_count, LS, heads_here, HD)
    kv_index = (first_head + jnp.arange(heads_here, dtype=jnp.int32)) // (H // KVH)
    keys_here = jnp.take(key_rows.reshape(cand_count, LS, KVH, HD), kv_index, axis=2)
    values_here = jnp.take(value_rows.reshape(cand_count, LS, KVH, HD), kv_index, axis=2)
    scores = (
        jnp.einsum("cthd,cuhd->chtu", own, keys_here, preferred_element_type=jnp.float32) * inv_root
    )
    positions = jnp.arange(LS, dtype=jnp.int32)
    causal = positions[None, :] <= positions[:, None]
    scores = jnp.where(causal[None, None], scores, -jnp.inf)
    suffix_peak = jnp.max(scores, axis=-1)
    weights = jnp.exp(scores - suffix_peak[..., None])
    suffix_sum = jnp.sum(weights, axis=-1)
    numerator = jnp.einsum(
        "chtu,cuhd->cthd",
        weights.astype(jnp.bfloat16),
        values_here,
        preferred_element_type=jnp.float32,
    )
    return (jnp.swapaxes(suffix_peak, 1, 2), jnp.swapaxes(suffix_sum, 1, 2), numerator)


def on_device(queries, suffix_keys, suffix_values, prefix_keys, prefix_values, lengths):
    cand_count = queries.shape[0]
    heads_here = queries.shape[2] // HD
    first_head = lax.axis_index("ctx") * heads_here
    gathered = lax.all_gather(queries, "ctx", axis=2, tiled=True)
    suffix_peak, suffix_sum, suffix_numerator = attend_suffix(
        queries, suffix_keys, suffix_values, first_head
    )
    peak_all, sum_all, partial_all = attend_prefix(gathered, prefix_keys, prefix_values)
    prefix_peak = lax.pmax(peak_all.astype(jnp.bfloat16), "ctx").astype(peak_all.dtype)
    block_weight = jnp.exp(peak_all - prefix_peak) * sum_all
    prefix_sum = lax.psum(block_weight, "ctx")
    weighted = (block_weight[..., None] * partial_all.astype(jnp.float32)).reshape(
        cand_count, LS, H * HD
    )
    summed = lax.psum_scatter(weighted, "ctx", scatter_dimension=2, tiled=True).reshape(
        cand_count, LS, heads_here, HD
    )
    own_peak = lax.dynamic_slice_in_dim(prefix_peak, first_head, heads_here, 2)
    own_sum = lax.dynamic_slice_in_dim(prefix_sum, first_head, heads_here, 2)
    highest = jnp.maximum(own_peak, suffix_peak)
    rescale = jnp.exp(own_peak - highest)
    numerator = summed * rescale[..., None]
    denominator = own_sum * rescale
    own_weight = jnp.exp(suffix_peak - highest)
    numerator = numerator + own_weight[..., None] * suffix_numerator
    denominator = denominator + own_weight * suffix_sum
    active = (jnp.arange(LS, dtype=jnp.int32)[None, :] < lengths[:, None])[..., None, None]
    mixed = jnp.where(active, numerator / denominator[..., None], 0.0)
    return mixed.reshape(cand_count, LS, heads_here * HD).astype(jnp.bfloat16)


def solution(mesh):
    in_specs = (
        P("cand", None, "ctx"),
        P("cand", None, None),
        P("cand", None, None),
        P("ctx", None),
        P("ctx", None),
        P("cand"),
    )
    out_specs = P("cand", None, "ctx")
    return jax.shard_map(
        on_device, mesh=mesh, in_specs=in_specs, out_specs=out_specs, check_vma=False
    )
```

profile of v0, /device:TPU:1, one launch (start us, length us, event | category | flops | bytes accessed | tf_op | source)
XLA Modules:
  0.0 281.3 jit_solution(14545065455759181504)
XLA Ops:
  6.5 1.7 copy.34
  8.3 2.9 %copy.36 = bf16[1024,1024]{0,1:T(8,128)(2,1)S(1)} copy(bf16[1024,1024]{1,0:T(8,128)(2,1)} %param.11) | data formatting | bytes 4194304 | tf_op args[3]
  11.1 4.0 %copy.52 = bf16[1024,1024]{0,1:T(8,128)(2,1)} copy(bf16[1024,1024]{1,0:T(8,128)(2,1)} %param.12) | data formatting | bytes 4194304 | tf_op args[4]
  15.1 64.2 %all-gather.2.cloned.1.call-done = bf16[1,128,8192]{1,2,0:T(8,128)(2,1)} async-done(((bf16[1,128,512]{1,2,0:T(8,128)(2,1)}), bf16[1,128,8192]{1,2,0:T(8,128)(2,1)}) %all-gather.2.cloned.1.call-update) | async-done | bytes 2097168 | tf_op jit(solution)/shard_map/all_gather | solution.py:79
  79.4 1.9 multiply_reduce_fusion.7
  81.3 0.8 multiply_reduce_fusion.6
  82.1 0.8 multiply_reduce_fusion.5
  82.9 0.8 multiply_reduce_fusion.4
  83.7 0.8 multiply_reduce_fusion.3
  84.5 0.8 multiply_reduce_fusion.2
  85.3 0.8 multiply_reduce_fusion.1
  86.9 0.9 fusion.1
  87.9 1.0 fusion.63
  88.9 0.9 fusion.3
  89.9 1.1 fusion.75
  91.0 0.9 fusion.5
  91.9 1.1 fusion.87
  93.0 0.9 fusion.7
  93.9 1.3 fusion.99
  95.2 0.9 fusion.9
  96.1 1.1 fusion.111
  97.2 0.9 fusion.11
  98.2 1.1 fusion.123
  99.3 0.9 fusion.13
  100.2 1.1 fusion.135
  101.3 0.9 fusion.15
  102.2 1.1 fusion.147
  103.4 61.4 %pmax.7 = bf16[1,128,64]{1,2,0:T(8,128)(2,1)S(1)} all-reduce(bf16[1,128,64]{1,2,0:T(8,128)(2,1)S(1)} %bitcast_convert_fusion), channel_id=1, replica_groups=mesh['ctx'=16,'cand'=32] {'ctx'}, use_global_device_ids=true, to_apply=%region_8.9 | all-reduce | flops 8192 | bytes 32768 | tf_op jit(solution)/shard_map/pmax | solution.py:84
  164.9 2.3 convert_multiply_fusion
  170.8 65.1 %psum.7 = f32[1,128,64]{1,2,0:T(8,128)S(1)} all-reduce(f32[1,128,64]{1,2,0:T(8,128)S(1)} %bitcast_multiply_fusion), channel_id=1, replica_groups=mesh['ctx'=16,'cand'=32] {'ctx'}, use_global_device_ids=true, to_apply=%region_19.21 | all-reduce | flops 8192 | bytes 65536 | tf_op jit(solution)/shard_map/psum | solution.py:86
  235.9 36.4 %reduce-scatter.2.cloned.1.call-done = f32[1,128,512]{1,2,0:T(8,128)} async-done(((f32[1,128,8192]{1,2,0:T(8,128)}), f32[1,128,512]{1,2,0:T(8,128)}) %reduce-scatter.2.cloned.1.call-update) | async-done | bytes 262160 | tf_op jit(solution)/shard_map/reduce_scatter | solution.py:90
  272.4 1.3 fusion.150
  (50 shorter events, 4.5 us)
Async XLA Ops:
  6.5 72.8 %all-gather.2.cloned.1.call-start = ((), (), s32[]{:S(2)}) async-start(), calls=%async_computation.1 | async-start | bytes 2228224 | tf_op jit(solution)/shard_map/all_gather | solution.py:79
  8.2 264.2 %reduce-scatter.2.cloned.1.call-start = ((), (), s32[]{:S(2)}) async-start(), calls=%async_computation.2 | async-start | bytes 4456448 | tf_op jit(solution)/shard_map/reduce_scatter | solution.py:90
  79.4 1.9 copy-start.1
  86.1 1.8 copy-start
  164.9 2.4 copy-start.2
  164.9 2.4 copy-start.3
  167.2 0.9 copy-start.4
Sparse Core Ops, SparseCore 0:
  10.7 68.6 all-gather.1
  167.4 104.9 reduce-scatter.1
where the time goes:
time: 282 us; the launch traced here: 281 us
  blocking collectives  127 us (45%)
  waiting for transfers between devices  101 us (36%)
  matrix products  17.9 us (6%)
  between operations  14.5 us (5%)
  local copies, waits for them, and re-layouts  11.7 us (4%)
  other arithmetic  9.84 us (3%)
    psum x1, blocking collectives, on_device(): prefix_sum = lax.psum(block_weight, 'ctx')  65.1 us
    all_gather x1, waiting for transfers between devices, on_device(): gathered = lax.all_gather(queries, 'ctx', axis=2, tiled=True)  64.2 us
    pmax x1, blocking collectives, on_device(): lax.pmax(peak_all.astype(jnp.bfloat16), 'ctx').astype(peak_all.dtype)  61.4 us
    reduce_scatter x1, waiting for transfers between devices, on_device(): lax.psum_scatter(weighted, 'ctx', scatter_dimension=2, tiled=True)  36.4 us
    unnamed x29, local copies, waits for them, and re-layouts  9.38 us
    dot_general x8, matrix products, attend_prefix(): jnp.einsum('ctgp,pd->ctgd', weights.astype(jnp.bfloat16), value_rows[:, k...  8.8 us
    dot_general x8, matrix products, attend_prefix(): jnp.einsum('ctgd,pd->ctgp', groups[:, :, kv_head], key_rows[:, kv_head],...  7.56 us
    reduce_sum x8, other arithmetic, attend_prefix(): block_sum = jnp.sum(weights, axis=-1)  7.35 us
  transfers between devices with their start and end apart: 2, of which 2 were waited for; matrix products, arithmetic and copies ran while one was open for 3% of the time, Pallas kernels for 0%

commit v1 on v0

v1 whole, which is shorter than its diff:
```python
import functools
import math

import jax
import jax.numpy as jnp
from jax import lax
from jax.experimental import pallas as pl
from jax.experimental.pallas import tpu as pltpu
from jax.sharding import PartitionSpec as P

H = 64
KVH = 8
HD = 128
LS = 128
P_DEV = 1024
NY = 4
HERE = 4
W = HERE * LS
ONES = 8

MESH = pl.DeviceIdType.MESH
NT = (((1,), (1,)), ((), ()))
TN = (((0,), (0,)), ((), ()))
SCALE = math.log2(math.e) / math.sqrt(HD)
F32 = jnp.float32
BF16 = jnp.bfloat16


def place():
    ctx, cand = lax.axis_index("ctx"), lax.axis_index("cand")
    return ctx // 4, (ctx // 2) % 2, ctx % 2, cand // 2, cand % 2


def device(y, half, core, z, low):
    return {"ctx": (y * 2 + half) * 2 + core, "cand": z * 2 + low}


def heads_in_rows(block):
    return jnp.concatenate([block[:, i * HD : (i + 1) * HD] for i in range(HERE)], axis=0)


def kernel(
    q_hbm, sk_hbm, sv_hbm, pk_hbm, pv_hbm, len_ref, out_ref,
    own_q, suffix_k, suffix_v, keys, values, values_t, queries, parts, part_stats, got, got_stats,
    suffix_sum, suffix_stats,
    own_sem, kv_sem, kv_send, kv_recv, q_sem, q_send, q_recv, o_send, o_recv, s_send, s_recv,
):
    y, half, core, z, low = place()
    half_c, low_c = (half + core) % 2, (low + core) % 2

    head = y * 2 + half
    columns = pl.ds(pl.multiple_of(head * HD, HD), HD)
    own_copies = [
        pltpu.make_async_copy(q_hbm, own_q, own_sem.at[0]),
        pltpu.make_async_copy(sk_hbm.at[:, columns], suffix_k, own_sem.at[1]),
        pltpu.make_async_copy(sv_hbm.at[:, columns], suffix_v, own_sem.at[2]),
    ]
    for copy in own_copies:
        copy.start()

    def order(i):
        return (y + jnp.where(i < 2, i, 5 - i)) % NY

    rows = pl.ds(pl.multiple_of(core * P_DEV, P_DEV), P_DEV)

    def kv_columns(item, parity):
        return pl.ds(pl.multiple_of((item * 2 + parity) * HD, HD), HD)

    def kv_local(item, j):
        src, dst = ((pk_hbm, keys), (pv_hbm, values))[j]
        return pltpu.make_async_copy(
            src.at[:, kv_columns(item, half_c)], dst.at[item, rows, :], kv_sem.at[item, j]
        )

    def kv_remote(item, j):
        src, dst = ((pk_hbm, keys), (pv_hbm, values))[j]
        return pltpu.make_async_remote_copy(
            src_ref=src.at[:, kv_columns(item, 1 - half_c)],
            dst_ref=dst.at[item, rows, :],
            send_sem=kv_send.at[item, j],
            recv_sem=kv_recv.at[item, j],
            device_id=device(y, half, 1 - core, z, low),
            device_id_type=MESH,
        )

    for i in range(NY):
        for j in range(2):
            kv_local(order(i), j).start()

    barrier = pltpu.get_barrier_semaphore()
    for dy in range(NY):
        for other in range(2):
            for c in range(2):
                if (dy, other, c) == (0, 0, 0):
                    continue
                pl.semaphore_signal(
                    barrier,
                    inc=1,
                    device_id=device(
                        (y + dy) % NY, (half + other) % 2, (core + c) % 2, z, (low + other) % 2
                    ),
                    device_id_type=MESH,
                )
    for copy in own_copies:
        copy.wait()
    pl.semaphore_wait(barrier, 15)

    def q_copy(dy, other):
        return pltpu.make_async_remote_copy(
            src_ref=own_q,
            dst_ref=queries.at[y, core],
            send_sem=q_send.at[dy, other],
            recv_sem=q_recv.at[y, core],
            device_id=device((y + dy) % NY, (half + other) % 2, other, z, (low + other) % 2),
            device_id_type=MESH,
        )

    q_local = pltpu.make_async_copy(q_hbm, queries.at[y, 0], q_sem)

    @pl.when(core == 0)
    def _():
        q_local.start()

    @pl.when(core == 1)
    def _():
        q_copy(0, 0).start()

    for j in range(2):
        kv_remote(order(0), j).start()
    q_copy(0, 1).start()
    for dy in (1, 3, 2):
        q_copy(dy, 0).start()
        q_copy(dy, 1).start()
    for i in range(1, NY):
        for j in range(2):
            kv_remote(order(i), j).start()

    q_rows = heads_in_rows(own_q[...])
    scores = lax.dot_general(suffix_k[...], q_rows, NT, preferred_element_type=F32)
    u = lax.broadcasted_iota(jnp.int32, (LS, W), 0)
    t = lax.broadcasted_iota(jnp.int32, (LS, W), 1) % LS
    scores = jnp.where(u <= t, scores, -1e30)
    peak = jnp.max(scores, axis=0, keepdims=True)
    probs = jnp.exp2((scores - peak) * SCALE)
    total = jnp.sum(probs, axis=0, keepdims=True)
    suffix_sum[...] = lax.dot_general(
        suffix_v[...], probs.astype(BF16), TN, preferred_element_type=F32
    )
    for i in range(HERE):
        suffix_stats[i : i + 1, :] = peak[:, i * LS : (i + 1) * LS]
        suffix_stats[HERE + i : HERE + i + 1, :] = total[:, i * LS : (i + 1) * LS]

    values_t[HD:, :] = jnp.ones((ONES, 2 * P_DEV), BF16)

    def out_copy(item, c):
        return pltpu.make_async_remote_copy(
            src_ref=parts.at[item, c],
            dst_ref=got.at[y * 2 + core],
            send_sem=o_send.at[item, c],
            recv_sem=o_recv.at[y * 2 + core],
            device_id=device(item, half_c, c, z, low_c),
            device_id_type=MESH,
        )

    def stat_copy(item, c):
        return pltpu.make_async_remote_copy(
            src_ref=part_stats.at[item, c],
            dst_ref=got_stats.at[y * 2 + core],
            send_sem=s_send.at[item, c],
            recv_sem=s_recv.at[y * 2 + core],
            device_id=device(item, half_c, c, z, low_c),
            device_id_type=MESH,
        )

    def one_item(i, carry):
        item = order(i)
        for j in range(2):
            kv_local(item, j).wait()
            kv_remote(item, j).wait_recv()
        values_t[:HD, :] = values[item].T
        for c in range(2):
            here = (i == 0) & (core == 0)

            if c == 0:

                @pl.when(here)
                def _():
                    q_local.wait()

                @pl.when(jnp.logical_not(here))
                def _():
                    pltpu.make_async_remote_copy(
                        src_ref=own_q, dst_ref=queries.at[item, 0], send_sem=q_send.at[0, 0],
                        recv_sem=q_recv.at[item, 0], device_id=device(y, half, 1 - core, z, low),
                        device_id_type=MESH,
                    ).wait_recv()

            else:
                pltpu.make_async_remote_copy(
                    src_ref=own_q, dst_ref=queries.at[item, 1], send_sem=q_send.at[0, 0],
                    recv_sem=q_recv.at[item, 1], device_id=device(y, half, 1 - core, z, low),
                    device_id_type=MESH,
                ).wait_recv()
            q_rows = heads_in_rows(queries[item, c])
            scores = lax.dot_general(keys[item], q_rows, NT, preferred_element_type=F32)
            peak = jnp.max(scores, axis=0, keepdims=True)
            probs = jnp.exp2((scores - peak) * SCALE).astype(BF16)
            both = jnp.dot(values_t[...], probs, preferred_element_type=F32)
            parts[item, c] = both[:HD].astype(BF16)
            for k in range(HERE):
                part_stats[item, c, k : k + 1, :] = peak[:, k * LS : (k + 1) * LS]
                part_stats[item, c, HERE + k : HERE + k + 1, :] = both[
                    HD : HD + 1, k * LS : (k + 1) * LS
                ]
            if c == 0:

                @pl.when(jnp.logical_not(here))
                def _():
                    out_copy(item, 0).start()
                    stat_copy(item, 0).start()

                @pl.when(here)
                def _():
                    got[y * 2] = parts[item, 0]
                    got_stats[y * 2] = part_stats[item, 0]

            else:
                out_copy(item, 1).start()
                stat_copy(item, 1).start()
        return carry

    lax.fori_loop(0, NY, one_item, 0)

    for dy in (0, 1, 3, 2):
        for c in range(2):
            slot = ((y + dy) % NY) * 2 + c

            def wait_slot(slot=slot):
                for buffer, source, send, recv in (
                    (got, parts, o_send, o_recv),
                    (got_stats, part_stats, s_send, s_recv),
                ):
                    pltpu.make_async_remote_copy(
                        src_ref=source.at[0, 0], dst_ref=buffer.at[slot], send_sem=send.at[0, 0],
                        recv_sem=recv.at[slot], device_id=device(y, half, 1 - core, z, low),
                        device_id_type=MESH,
                    ).wait_recv()

            if (dy, c) == (0, 0):
                pl.when(core == 1)(wait_slot)
            else:
                wait_slot()

    live = lax.broadcasted_iota(jnp.int32, (LS, HD), 0) < len_ref[0]
    for k in range(HERE):
        lanes = slice(k * LS, (k + 1) * LS)
        own_peak = suffix_stats[k : k + 1, :]
        peaks = [got_stats[s, k : k + 1, :] for s in range(2 * NY)]
        highest = functools.reduce(jnp.maximum, peaks, own_peak)
        weight = jnp.exp2((own_peak - highest) * SCALE)
        over = suffix_sum[:, lanes] * weight
        under = suffix_stats[HERE + k : HERE + k + 1, :] * weight
        for s in range(2 * NY):
            weight = jnp.exp2((peaks[s] - highest) * SCALE)
            over = over + got[s, :, lanes].astype(F32) * weight
            under = under + got_stats[s, HERE + k : HERE + k + 1, :] * weight
        mixed = (over / under).T
        out_ref[:, k * HD : (k + 1) * HD] = jnp.where(live, mixed, 0.0).astype(BF16)

    @pl.when(core == 1)
    def _():
        q_copy(0, 0).wait_send()

    q_copy(0, 1).wait_send()
    for dy in (1, 3, 2):
        q_copy(dy, 0).wait_send()
        q_copy(dy, 1).wait_send()
    for i in range(NY):
        for j in range(2):
            kv_remote(order(i), j).wait_send()
        for c in range(2):

            def wait_sent(i=i, c=c):
                out_copy(order(i), c).wait_send()
                stat_copy(order(i), c).wait_send()

            if (i, c) == (0, 0):
                pl.when(core == 1)(wait_sent)
            else:
                wait_sent()


def on_device(queries, suffix_keys, suffix_values, prefix_keys, prefix_values, lengths):
    hbm = pl.BlockSpec(memory_space=pl.ANY)
    dma = pltpu.SemaphoreType.DMA
    out = pl.pallas_call(
        kernel,
        name="attend",
        out_shape=jax.ShapeDtypeStruct((LS, HERE * HD), BF16),
        in_specs=[hbm] * 5 + [pl.BlockSpec(memory_space=pltpu.SMEM)],
        out_specs=pl.BlockSpec(memory_space=pltpu.VMEM),
        scratch_shapes=[
            pltpu.VMEM((LS, HERE * HD), BF16),
            pltpu.VMEM((LS, HD), BF16),
            pltpu.VMEM((LS, HD), BF16),
            pltpu.VMEM((NY, 2 * P_DEV, HD), BF16),
            pltpu.VMEM((NY, 2 * P_DEV, HD), BF16),
            pltpu.VMEM((HD + ONES, 2 * P_DEV), BF16),
            pltpu.VMEM((NY, 2, LS, HERE * HD), BF16),
            pltpu.VMEM((NY, 2, HD, W), BF16),
            pltpu.VMEM((NY, 2, 2 * HERE, LS), F32),
            pltpu.VMEM((2 * NY, HD, W), BF16),
            pltpu.VMEM((2 * NY, 2 * HERE, LS), F32),
            pltpu.VMEM((HD, W), F32),
            pltpu.VMEM((2 * HERE, LS), F32),
            dma((3,)),
            dma((NY, 2)),
            dma((NY, 2)),
            dma((NY, 2)),
            dma,
            dma((NY, 2)),
            dma((NY, 2)),
            dma((NY, 2)),
            dma((2 * NY,)),
            dma((NY, 2)),
            dma((2 * NY,)),
        ],
        compiler_params=pltpu.CompilerParams(
            collective_id=0, has_side_effects=True, vmem_limit_bytes=62 * 2**20
        ),
        cost_estimate=pl.CostEstimate(
            flops=4 * 8192 * 1024 * 128, bytes_accessed=6 * 2**20, transcendentals=8192 * 1024
        ),
    )(
        queries.reshape(LS, HERE * HD),
        suffix_keys.reshape(LS, KVH * HD),
        suffix_values.reshape(LS, KVH * HD),
        prefix_keys,
        prefix_values,
        lengths,
    )
    return out.reshape(1, LS, HERE * HD)


def solution(mesh):
    in_specs = (
        P("cand", None, "ctx"),
        P("cand", None, None),
        P("cand", None, None),
        P("ctx", None),
        P("ctx", None),
        P("cand"),
    )
    return jax.shard_map(
        on_device, mesh=mesh, in_specs=in_specs, out_specs=P("cand", None, "ctx"), check_vma=False
    )
```

time: 282 us -> 41.2 us (0.15)
  blocking collectives: 127 us -> 0 us
  waiting for transfers between devices: 101 us -> 0 us
  Pallas kernels: 0 us -> 38.8 us
  matrix products: 17.9 us -> 0 us
  between operations: 14.5 us -> 0.66 us
  local copies, waits for them, and re-layouts: 11.7 us -> 1.57 us
  other arithmetic: 9.84 us -> 0 us
    psum x1 -> x0, blocking collectives: 65.1 us -> none  [on_device(): prefix_sum = lax.psum(block_weight, 'ctx')]
    all_gather x1 -> x0, waiting for transfers between devices: 64.2 us -> none  [on_device(): gathered = lax.all_gather(queries, 'ctx', axis=2, tiled=True)]
    pmax x1 -> x0, blocking collectives: 61.4 us -> none  [on_device(): lax.pmax(peak_all.astype(jnp.bfloat16), 'ctx').astype(peak_all.dtype)]
    pallas_call x0 -> x1, Pallas kernels: none -> 38.8 us  [on_device(): pl.pallas_call(kernel, name='attend', out_shape=jax.ShapeDtypeStruct((LS,...]
    reduce_scatter x1 -> x0, waiting for transfers between devices: 36.4 us -> none  [on_device(): lax.psum_scatter(weighted, 'ctx', scatter_dimension=2, tiled=True)]
    dot_general x18 -> x0, matrix products: 17.9 us -> none  [the longest x8 8.8 us: attend_prefix(): jnp.einsum('ctgp,pd->ctgd', weights.astype(jnp.bfloat16), value_rows[:, k...]
    unnamed x29 -> x1, local copies, waits for them, and re-layouts: 9.38 us -> 1.57 us
    reduce_sum x9 -> x0, other arithmetic: 7.41 us -> none  [the longest x8 7.35 us: attend_prefix(): block_sum = jnp.sum(weights, axis=-1)]
  transfers between devices with their start and end apart: 2 -> 0, of which waited for: 2 -> 0; matrix products, arithmetic and copies ran while one was open for 3% -> 0% of each run, Pallas kernels for 0% -> 0%
where the time goes in v1:
time: 41.2 us; the launch traced here: 41 us
  Pallas kernels  38.8 us (94%)
  local copies, waits for them, and re-layouts  1.57 us (4%)
  between operations  0.66 us (2%)
    pallas_call x1, Pallas kernels, on_device(): pl.pallas_call(kernel, name='attend', out_shape=jax.ShapeDtypeStruct((LS,...  38.8 us
    unnamed x1, local copies, waits for them, and re-layouts  1.57 us

profile of v1, /device:TPU:1, one launch (start us, length us, event | category | flops | bytes accessed | tf_op | source)
XLA Modules:
  0.0 41.0 jit_solution(3125407987627642268)
XLA Ops:
  0.7 38.8 %attend.1 = bf16[128,512]{1,0:T(8,128)(2,1)} custom-call(bf16[128,512]{1,0:T(8,128)(2,1)} %bitcast.7, bf16[128,1024]{1,0:T(8,128)(2,1)} %bitcast.5, bf16[128,1024]{1,0:T(8,128)(2,1)} %bitcast.6, bf16[1024,1024]{1,0:T(8,128)(2,1)} %pk_hbm.1, bf16[1024,1024]{1,0:T(8,128)(2,1)} %pv_hbm.1, s32[1]{0:T(128)S(6)} %copy.8.len_ref), custom_call_target="tpu_custom_call" | custom-call | flops 4294967296 | bytes 6291456 | tf_op jit(solution)/shard_map/attend/pallas_call | solution.py:296
  39.5 1.6 %copy.9 = bf16[1,128,512]{2,1,0:T(8,128)(2,1)} copy(bf16[1,128,512]{2,1,0:T(8,128)(2,1)} %bitcast.4) | data formatting | bytes 262144

commit v2 on v0

v2 whole, which is shorter than its diff:
```python
import functools
import math

import jax
import jax.numpy as jnp
from jax import lax
from jax.experimental import pallas as pl
from jax.experimental.pallas import tpu as pltpu
from jax.sharding import PartitionSpec as P

H = 64
KVH = 8
HD = 128
LS = 128
P_DEV = 1024
NY = 4
HERE = 4
W = HERE * LS
TILES = 8
KEYS = 2 * P_DEV
CHUNK = 512
STEP = (0, -1, 2, 1, -1, 2, 0, 1)
SIDE = (0, 0, 0, 1, 1, 1, 1, 0)
SENT_TO = (0, 0, 0, 0, 0, 1, 1, 0)
MIRROR = (0, 7, 2, 4, 3, 5, 6, 1)
ONES = 8


MESH = pl.DeviceIdType.MESH
NT = (((1,), (1,)), ((), ()))
TN = (((0,), (0,)), ((), ()))
SCALE = math.log2(math.e) / math.sqrt(HD)
F32 = jnp.float32
BF16 = jnp.bfloat16


def place():
    ctx, cand = lax.axis_index("ctx"), lax.axis_index("cand")
    return ctx // 4, (ctx // 2) % 2, ctx % 2, cand // 2, cand % 2


def heads_in_rows(block):
    return jnp.concatenate([block[:, i * HD : (i + 1) * HD] for i in range(HERE)], axis=0)


def kernel(
    q_hbm, sk_hbm, sv_hbm, pk_hbm, pv_hbm, len_ref, out_ref,
    own_q, suffix_k, suffix_v, keys, values, values_t, queries, scores, probs, parts, part_stats, got, got_stats,
    total, stats,
    own_sem, kv_sem, kv_send, kv_recv, q_send, q_recv, o_send, o_recv, s_send, s_recv,
):
    y, half, core, z, low = place()

    onward = 1 - 2 * core

    def device(step, other, c):
        return {
            "ctx": (((y + NY + step * onward) % NY) * 2 + (half + other) % 2) * 2 + c,
            "cand": z * 2 + (low + other) % 2,
        }

    def pick(table, t):
        if isinstance(t, int):
            return table[t]
        return functools.reduce(lambda x, k: jnp.where(t == k, table[k], x), range(1, TILES), table[0])

    def remote(src, dst, send, recv, target):
        return pltpu.make_async_remote_copy(
            src_ref=src, dst_ref=dst, send_sem=send, recv_sem=recv, device_id=target, device_id_type=MESH
        )

    columns = pl.ds(pl.multiple_of((y * 2 + half) * HD, HD), HD)
    own_copies = [
        pltpu.make_async_copy(q_hbm, own_q, own_sem.at[0]),
        pltpu.make_async_copy(sk_hbm.at[:, columns], suffix_k, own_sem.at[1]),
        pltpu.make_async_copy(sv_hbm.at[:, columns], suffix_v, own_sem.at[2]),
    ]
    own, other_core = slice(0, P_DEV), slice(P_DEV, KEYS)

    def kv_local(t, j):
        kv_head = ((y + NY + STEP[t] * onward) % NY) * 2 + (half + SIDE[t]) % 2
        cols = pl.ds(pl.multiple_of(kv_head * HD, HD), HD)
        src, dst = ((pk_hbm, keys), (pv_hbm, values))[j]
        return pltpu.make_async_copy(src.at[:, cols], dst.at[t, own, :], kv_sem.at[t, j])

    def kv_remote(t, j):
        ref = (keys, values)[j]
        return remote(
            ref.at[pick(MIRROR, t), own, :], ref.at[t, other_core, :], kv_send.at[t, j], kv_recv.at[t, j],
            device(0, 0, 1 - core),
        )

    barrier = pltpu.get_barrier_semaphore()
    for dy, other, c in ((0, 0, 1 - core), (0, 1, core), (1, 0, core), (-1, 0, core)):
        pl.semaphore_signal(barrier, inc=1, device_id=device(dy, other, c), device_id_type=MESH)

    for j in range(2):
        kv_local(0, j).start()
    for copy in own_copies:
        copy.start()
    for t in (1, 7):
        for j in range(2):
            kv_local(t, j).start()
    pl.semaphore_wait(barrier, 4)

    def q_copy(src, n, slot, step, other):
        return remote(src, queries.at[slot], q_send.at[n], q_recv.at[slot], device(step, other, core))

    q_copies = [
        q_copy(q_hbm, 0, 1, 1, 0),
        q_copy(q_hbm, 1, 6, 0, 1),
        q_copy(q_hbm, 2, 7, -1, 0),
        q_copy(queries.at[1], 3, 2, 1, 0),
        q_copy(queries.at[1], 4, 4, 0, 1),
        q_copy(queries.at[6], 5, 3, -1, 0),
        q_copy(queries.at[2], 6, 5, 0, 1),
    ]

    def q_arrived(t):
        remote(own_q, queries.at[t], q_send.at[0], q_recv.at[t], device(0, 0, 1 - core)).wait_recv()

    def kv_arrived(t):
        for j in range(2):
            kv_remote(t, j).wait_recv()

    def kv_out(t):
        for j in range(2):
            if t <= MIRROR[t]:
                for m in sorted({t, MIRROR[t]}):
                    kv_local(m, j).wait()
            kv_remote(t, j).start()

    q_copies[0].start()
    q_copies[1].start()
    kv_out(0)
    for t in range(2, 7):
        for j in range(2):
            kv_local(t, j).start()
    kv_out(1)

    for copy in own_copies:
        copy.wait()
    q_rows = heads_in_rows(own_q[...])
    s = lax.dot_general(suffix_k[...], q_rows, NT, preferred_element_type=F32)
    u = lax.broadcasted_iota(jnp.int32, (LS, W), 0)
    t = lax.broadcasted_iota(jnp.int32, (LS, W), 1) % LS
    s = jnp.where(u <= t, s, -1e30)
    peak = jnp.max(s, axis=0, keepdims=True)
    p = jnp.exp2((s - peak) * SCALE)
    under = jnp.sum(p, axis=0, keepdims=True)
    total[...] = lax.dot_general(suffix_v[...], p.astype(BF16), TN, preferred_element_type=F32)
    for i in range(HERE):
        stats[i : i + 1, :] = peak[:, i * LS : (i + 1) * LS]
        stats[HERE + i : HERE + i + 1, :] = under[:, i * LS : (i + 1) * LS]

    q_copies[0].wait_send()
    q_copies[2].start()

    for i in range(2):
        values_t[i, HD:, :] = jnp.ones((ONES, KEYS), BF16)
    queries[0] = own_q[...]

    def out_copies(t):
        target = device(pick(STEP, t), pick(SENT_TO, t), core)
        return [
            remote(parts.at[t], got.at[t], o_send.at[t], o_recv.at[t], target),
            remote(part_stats.at[t], got_stats.at[t], s_send.at[t], s_recv.at[t], target),
        ]

    def finish(t, peak, sums, lanes):
        parts[t, :, lanes] = sums[:HD].astype(BF16)
        for k in range(lanes.start // LS, lanes.stop // LS):
            at = slice(k * LS, (k + 1) * LS)
            part_stats[t, k : k + 1, :] = peak[:, at]
            part_stats[t, HERE + k : HERE + k + 1, :] = sums[
                HD : HD + 1, k * LS - lanes.start : (k + 1) * LS - lanes.start
            ]

    def score(i, t, q_rows, at):
        s = lax.dot_general(keys[t, at, :], q_rows, NT, preferred_element_type=F32)
        scores[i, at, :] = s
        return jnp.max(s, axis=0, keepdims=True)

    def soften(i, peak, at):
        probs[i, at, :] = jnp.exp2((scores[i, at, :] - peak) * SCALE).astype(BF16)

    chunks = [slice(k, k + CHUNK) for k in range(0, KEYS, CHUNK)]

    def pair(i, carry):
        a, b = 2 * i, 2 * i + 1
        kv_arrived(a)

        @pl.when(i == 0)
        def _():
            kv_out(2)
            kv_out(3)

        @pl.when(i == 1)
        def _():
            kv_out(6)
            kv_out(7)
            q_arrived(2)
            q_copies[6].start()

        @pl.when(i == 2)
        def _():
            q_arrived(4)

        q_rows = heads_in_rows(queries[a])
        peak = functools.reduce(jnp.maximum, [score(0, a, q_rows, at) for at in chunks])
        values_t[0, :HD, :] = values[a].T
        kv_arrived(b)

        @pl.when(i == 0)
        def _():
            q_arrived(1)
            q_copies[3].start()
            q_copies[4].start()
            kv_out(4)
            kv_out(5)

        @pl.when(i == 1)
        def _():
            q_arrived(3)

        @pl.when(i == 2)
        def _():
            q_arrived(5)

        @pl.when(i == 3)
        def _():
            q_arrived(7)

        q_rows = heads_in_rows(queries[b])
        peak_b = []
        for at in chunks:
            peak_b.append(score(1, b, q_rows, at))
            soften(0, peak, at)
        peak_b = functools.reduce(jnp.maximum, peak_b)
        values_t[1, :HD, :] = values[b].T

        @pl.when(i == 0)
        def _():
            q_arrived(6)
            q_copies[5].start()

        for n in range(2):
            lanes = slice(n * W // 2, (n + 1) * W // 2)
            sums = jnp.dot(values_t[0], probs[0, :, lanes], preferred_element_type=F32)
            finish(a, peak, sums, lanes)
            for at in chunks[2 * n : 2 * n + 2]:
                soften(1, peak_b, at)

        @pl.when((i == 1) | (i == 2))
        def _():
            for copy in out_copies(a):
                copy.start()

        sums = jnp.dot(values_t[1], probs[1], preferred_element_type=F32)
        finish(b, peak_b, sums, slice(0, W))
        for copy in out_copies(b):
            copy.start()

        return carry

    lax.fori_loop(0, TILES // 2, pair, 0)

    def add(pieces, k):
        lanes = slice(k * LS, (k + 1) * LS)
        peaks = [at[k : k + 1, :] for _, at in pieces]
        highest = functools.reduce(jnp.maximum, peaks)
        over, under = 0.0, 0.0
        for (part, at), peak in zip(pieces, peaks, strict=True):
            weight = jnp.exp2((peak - highest) * SCALE)
            over = over + part[:, lanes].astype(F32) * weight
            under = under + at[HERE + k : HERE + k + 1, :] * weight
        return over, under, highest

    def fold(pieces, part, at):
        for k in range(HERE):
            over, under, highest = add(pieces, k)
            part[:, k * LS : (k + 1) * LS] = over.astype(part.dtype)
            at[k : k + 1, :] = highest
            at[HERE + k : HERE + k + 1, :] = under

    def arrived(ts):
        for t in ts:
            for copy in out_copies(t):
                copy.wait_recv()
        return [(got.at[t], got_stats.at[t]) for t in ts]

    near = parts.at[6], part_stats.at[6]
    fold([near] + arrived((3, 4)), *near)
    for copy in out_copies(6):
        copy.start()
    so_far = total, stats
    fold([so_far, (parts.at[0], part_stats.at[0])] + arrived((1, 2)), *so_far)
    pieces = [so_far] + arrived((7, 5, 6))
    live = lax.broadcasted_iota(jnp.int32, (LS, HD), 0) < len_ref[0]
    for k in range(HERE):
        over, under, _ = add(pieces, k)
        mixed = (over * (1.0 / under)).T
        out_ref[:, k * HD : (k + 1) * HD] = jnp.where(live, mixed, 0.0).astype(BF16)

    for copy in q_copies[1:]:
        copy.wait_send()
    for t in range(TILES):
        for j in range(2):
            kv_remote(t, j).wait_send()
        if t > 0:
            for copy in out_copies(t):
                copy.wait_send()


def on_device(queries, suffix_keys, suffix_values, prefix_keys, prefix_values, lengths):
    hbm = pl.BlockSpec(memory_space=pl.ANY)
    dma = pltpu.SemaphoreType.DMA
    out = pl.pallas_call(
        kernel,
        name="attend",
        out_shape=jax.ShapeDtypeStruct((LS, HERE * HD), BF16),
        in_specs=[hbm] * 5 + [pl.BlockSpec(memory_space=pltpu.SMEM)],
        out_specs=pl.BlockSpec(memory_space=pltpu.VMEM),
        scratch_shapes=[
            pltpu.VMEM((LS, HERE * HD), BF16),
            pltpu.VMEM((LS, HD), BF16),
            pltpu.VMEM((LS, HD), BF16),
            pltpu.VMEM((TILES, KEYS, HD), BF16),
            pltpu.VMEM((TILES, KEYS, HD), BF16),
            pltpu.VMEM((2, HD + ONES, KEYS), BF16),
            pltpu.VMEM((TILES, LS, HERE * HD), BF16),
            pltpu.VMEM((2, KEYS, W), F32),
            pltpu.VMEM((2, KEYS, W), BF16),
            pltpu.VMEM((TILES, HD, W), BF16),
            pltpu.VMEM((TILES, 2 * HERE, LS), F32),
            pltpu.VMEM((TILES, HD, W), BF16),
            pltpu.VMEM((TILES, 2 * HERE, LS), F32),
            pltpu.VMEM((HD, W), F32),
            pltpu.VMEM((2 * HERE, LS), F32),
            dma((3,)),
            dma((TILES, 2)),
            dma((TILES, 2)),
            dma((TILES, 2)),
            dma((7,)),
            dma((TILES,)),
            dma((TILES,)),
            dma((TILES,)),
            dma((TILES,)),
            dma((TILES,)),
        ],
        compiler_params=pltpu.CompilerParams(
            collective_id=0, has_side_effects=True, vmem_limit_bytes=62 * 2**20
        ),
        cost_estimate=pl.CostEstimate(
            flops=4 * 8192 * 1024 * 128, bytes_accessed=6 * 2**20, transcendentals=8192 * 1024
        ),
    )(
        queries.reshape(LS, HERE * HD),
        suffix_keys.reshape(LS, KVH * HD),
        suffix_values.reshape(LS, KVH * HD),
        prefix_keys,
        prefix_values,
        lengths,
    )
    return out.reshape(1, LS, HERE * HD)


def solution(mesh):
    in_specs = (
        P("cand", None, "ctx"),
        P("cand", None, None),
        P("cand", None, None),
        P("ctx", None),
        P("ctx", None),
        P("cand"),
    )
    return jax.shard_map(
        on_device, mesh=mesh, in_specs=in_specs, out_specs=P("cand", None, "ctx"), check_vma=False
    )
```

time: 282 us -> 39.5 us (0.14)
  blocking collectives: 127 us -> 0 us
  waiting for transfers between devices: 101 us -> 0 us
  Pallas kernels: 0 us -> 37.1 us
  matrix products: 17.9 us -> 0 us
  between operations: 14.5 us -> 0.66 us
  local copies, waits for them, and re-layouts: 11.7 us -> 1.57 us
  other arithmetic: 9.84 us -> 0 us
    psum x1 -> x0, blocking collectives: 65.1 us -> none  [on_device(): prefix_sum = lax.psum(block_weight, 'ctx')]
    all_gather x1 -> x0, waiting for transfers between devices: 64.2 us -> none  [on_device(): gathered = lax.all_gather(queries, 'ctx', axis=2, tiled=True)]
    pmax x1 -> x0, blocking collectives: 61.4 us -> none  [on_device(): lax.pmax(peak_all.astype(jnp.bfloat16), 'ctx').astype(peak_all.dtype)]
    pallas_call x0 -> x1, Pallas kernels: none -> 37.1 us  [on_device(): pl.pallas_call(kernel, name='attend', out_shape=jax.ShapeDtypeStruct((LS,...]
    reduce_scatter x1 -> x0, waiting for transfers between devices: 36.4 us -> none  [on_device(): lax.psum_scatter(weighted, 'ctx', scatter_dimension=2, tiled=True)]
    dot_general x18 -> x0, matrix products: 17.9 us -> none  [the longest x8 8.8 us: attend_prefix(): jnp.einsum('ctgp,pd->ctgd', weights.astype(jnp.bfloat16), value_rows[:, k...]
    unnamed x29 -> x1, local copies, waits for them, and re-layouts: 9.38 us -> 1.57 us
    reduce_sum x9 -> x0, other arithmetic: 7.41 us -> none  [the longest x8 7.35 us: attend_prefix(): block_sum = jnp.sum(weights, axis=-1)]
  transfers between devices with their start and end apart: 2 -> 0, of which waited for: 2 -> 0; matrix products, arithmetic and copies ran while one was open for 3% -> 0% of each run, Pallas kernels for 0% -> 0%
where the time goes in v2:
time: 39.5 us; the launch traced here: 39.3 us
  Pallas kernels  37.1 us (94%)
  local copies, waits for them, and re-layouts  1.57 us (4%)
  between operations  0.66 us (2%)
    pallas_call x1, Pallas kernels, on_device(): pl.pallas_call(kernel, name='attend', out_shape=jax.ShapeDtypeStruct((LS,...  37.1 us
    unnamed x1, local copies, waits for them, and re-layouts  1.57 us

profile of v2, /device:TPU:1, one launch (start us, length us, event | category | flops | bytes accessed | tf_op | source)
XLA Modules:
  0.0 39.3 jit_solution(3141277918690621376)
XLA Ops:
  0.7 37.1 %attend.1 = bf16[128,512]{1,0:T(8,128)(2,1)} custom-call(bf16[128,512]{1,0:T(8,128)(2,1)} %bitcast.7, bf16[128,1024]{1,0:T(8,128)(2,1)} %bitcast.5, bf16[128,1024]{1,0:T(8,128)(2,1)} %bitcast.6, bf16[1024,1024]{1,0:T(8,128)(2,1)} %pk_hbm.1, bf16[1024,1024]{1,0:T(8,128)(2,1)} %pv_hbm.1, s32[1]{0:T(128)S(6)} %copy.8.len_ref), custom_call_target="tpu_custom_call" | custom-call | flops 4294967296 | bytes 6291456 | tf_op jit(solution)/shard_map/attend/pallas_call | solution.py:318
  37.7 1.6 %copy.9 = bf16[1,128,512]{2,1,0:T(8,128)(2,1)} copy(bf16[1,128,512]{2,1,0:T(8,128)(2,1)} %bitcast.4) | data formatting | bytes 262144

commit v3 on v2

--- a/solution.py
+++ b/solution.py
@@ -156,8 +156,7 @@
     q_copies[0].wait_send()
     q_copies[2].start()
 
-    for i in range(2):
-        values_t[i, HD:, :] = jnp.ones((ONES, KEYS), BF16)
+    values_t[HD:, :] = jnp.ones((ONES, KEYS), BF16)
     queries[0] = own_q[...]
 
     def out_copies(t):
@@ -167,103 +166,83 @@
             remote(part_stats.at[t], got_stats.at[t], s_send.at[t], s_recv.at[t], target),
         ]
 
-    def finish(t, peak, sums, lanes):
-        parts[t, :, lanes] = sums[:HD].astype(BF16)
-        for k in range(lanes.start // LS, lanes.stop // LS):
-            at = slice(k * LS, (k + 1) * LS)
-            part_stats[t, k : k + 1, :] = peak[:, at]
-            part_stats[t, HERE + k : HERE + k + 1, :] = sums[
-                HD : HD + 1, k * LS - lanes.start : (k + 1) * LS - lanes.start
-            ]
-
-    def score(i, t, q_rows, at):
-        s = lax.dot_general(keys[t, at, :], q_rows, NT, preferred_element_type=F32)
-        scores[i, at, :] = s
-        return jnp.max(s, axis=0, keepdims=True)
-
-    def soften(i, peak, at):
-        probs[i, at, :] = jnp.exp2((scores[i, at, :] - peak) * SCALE).astype(BF16)
-
     chunks = [slice(k, k + CHUNK) for k in range(0, KEYS, CHUNK)]
-
-    def pair(i, carry):
-        a, b = 2 * i, 2 * i + 1
-        kv_arrived(a)
-
-        @pl.when(i == 0)
+    halves = [slice(0, W // 2), slice(W // 2, W)]
+
+    def tile(t, carry):
+        kv_arrived(t)
+
+        @pl.when(t == 0)
         def _():
             kv_out(2)
             kv_out(3)
 
-        @pl.when(i == 1)
-        def _():
+        @pl.when(t == 1)
+        def _():
+            kv_out(4)
+            kv_out(5)
+
+        @pl.when(t == 2)
+        def _():
+            q_arrived(2)
+            q_copies[6].start()
             kv_out(6)
             kv_out(7)
-            q_arrived(2)
-            q_copies[6].start()
-
-        @pl.when(i == 2)
-        def _():
-            q_arrived(4)
-
-        q_rows = heads_in_rows(queries[a])
-        peak = functools.reduce(jnp.maximum, [score(0, a, q_rows, at) for at in chunks])
-        values_t[0, :HD, :] = values[a].T
-        kv_arrived(b)
-
-        @pl.when(i == 0)
+
+        @pl.when((t == 3) | (t == 4) | (t == 5) | (t == 7))
+        def _():
+            q_arrived(t)
+
+        q_rows = heads_in_rows(queries[t])
+
+        def score(n, at):
+            s = lax.dot_general(keys[t, at, :], q_rows[halves[n]], NT, preferred_element_type=F32)
+            scores[at, halves[n]] = s
+            return jnp.max(s, axis=0, keepdims=True)
+
+        def soften(n, peak, at):
+            probs[at, halves[n]] = jnp.exp2((scores[at, halves[n]] - peak) * SCALE).astype(BF16)
+
+        def finish(n, peak):
+            sums = jnp.dot(values_t[...], probs[:, halves[n]], preferred_element_type=F32)
+            parts[t, :, halves[n]] = sums[:HD].astype(BF16)
+            for k in range(HERE // 2):
+                at, head = slice(k * LS, (k + 1) * LS), n * HERE // 2 + k
+                part_stats[t, head : head + 1, :] = peak[:, at]
+                part_stats[t, HERE + head : HERE + head + 1, :] = sums[HD : HD + 1, at]
+
+        peak = functools.reduce(jnp.maximum, [score(0, at) for at in chunks])
+        values_t[:HD, :] = values[t].T
+        next_peak = []
+        for at in chunks:
+            next_peak.append(score(1, at))
+            soften(0, peak, at)
+        next_peak = functools.reduce(jnp.maximum, next_peak)
+
+        @pl.when(t == 0)
         def _():
             q_arrived(1)
             q_copies[3].start()
             q_copies[4].start()
-            kv_out(4)
-            kv_out(5)
-
-        @pl.when(i == 1)
-        def _():
-            q_arrived(3)
-
-        @pl.when(i == 2)
-        def _():
-            q_arrived(5)
-
-        @pl.when(i == 3)
-        def _():
-            q_arrived(7)
-
-        q_rows = heads_in_rows(queries[b])
-        peak_b = []
+
+        finish(0, peak)
         for at in chunks:
-            peak_b.append(score(1, b, q_rows, at))
-            soften(0, peak, at)
-        peak_b = functools.reduce(jnp.maximum, peak_b)
-        values_t[1, :HD, :] = values[b].T
-
-        @pl.when(i == 0)
+            soften(1, next_peak, at)
+        finish(1, next_peak)
+
+        @pl.when((t != 0) & (t != 6))
+        def _():
+            for copy in out_copies(t):
+                copy.start()
+
+        @pl.when(t == 1)
         def _():
             q_arrived(6)
             q_copies[5].start()
 
-        for n in range(2):
-            lanes = slice(n * W // 2, (n + 1) * W // 2)
-            sums = jnp.dot(values_t[0], probs[0, :, lanes], preferred_element_type=F32)
-            finish(a, peak, sums, lanes)
-            for at in chunks[2 * n : 2 * n + 2]:
-                soften(1, peak_b, at)
-
-        @pl.when((i == 1) | (i == 2))
-        def _():
-            for copy in out_copies(a):
-                copy.start()
-
-        sums = jnp.dot(values_t[1], probs[1], preferred_element_type=F32)
-        finish(b, peak_b, sums, slice(0, W))
-        for copy in out_copies(b):
-            copy.start()
-
         return carry
 
-    lax.fori_loop(0, TILES // 2, pair, 0)
+    lax.fori_loop(0, TILES, tile, 0)
 
     def add(pieces, k):
         lanes = slice(k * LS, (k + 1) * LS)
@@ -327,10 +306,10 @@
             pltpu.VMEM((LS, HD), BF16),
             pltpu.VMEM((TILES, KEYS, HD), BF16),
             pltpu.VMEM((TILES, KEYS, HD), BF16),
-            pltpu.VMEM((2, HD + ONES, KEYS), BF16),
+            pltpu.VMEM((HD + ONES, KEYS), BF16),
             pltpu.VMEM((TILES, LS, HERE * HD), BF16),
-            pltpu.VMEM((2, KEYS, W), F32),
-            pltpu.VMEM((2, KEYS, W), BF16),
+            pltpu.VMEM((KEYS, W), F32),
+            pltpu.VMEM((KEYS, W), BF16),
             pltpu.VMEM((TILES, HD, W), BF16),
             pltpu.VMEM((TILES, 2 * HERE, LS), F32),
             pltpu.VMEM((TILES, HD, W), BF16),

time: 39.5 us -> 37.9 us (0.959)
  the two profiles are of different devices: /device:TPU:1 before, /device:TPU:22 now
where the time goes in v3:
time: 37.9 us; the launch traced here: 37.8 us
  Pallas kernels  35.5 us (94%)
  local copies, waits for them, and re-layouts  1.57 us (4%)
  between operations  0.66 us (2%)
    pallas_call x1, Pallas kernels, on_device(): pl.pallas_call(kernel, name='attend', out_shape=jax.ShapeDtypeStruct((LS,...  35.5 us
    unnamed x1, local copies, waits for them, and re-layouts  1.57 us

profile of v3, /device:TPU:22, one launch (start us, length us, event | category | flops | bytes accessed | tf_op | source)
XLA Modules:
  0.0 37.8 jit_solution(10098079895068978603)
XLA Ops:
  0.7 35.5 %attend.1 = bf16[128,512]{1,0:T(8,128)(2,1)} custom-call(bf16[128,512]{1,0:T(8,128)(2,1)} %bitcast.7, bf16[128,1024]{1,0:T(8,128)(2,1)} %bitcast.5, bf16[128,1024]{1,0:T(8,128)(2,1)} %bitcast.6, bf16[1024,1024]{1,0:T(8,128)(2,1)} %pk_hbm.1, bf16[1024,1024]{1,0:T(8,128)(2,1)} %pv_hbm.1, s32[1]{0:T(128)S(6)} %copy.8.len_ref), custom_call_target="tpu_custom_call" | custom-call | flops 4294967296 | bytes 6291456 | tf_op jit(solution)/shard_map/attend/pallas_call | solution.py:297
  36.2 1.6 %copy.9 = bf16[1,128,512]{2,1,0:T(8,128)(2,1)} copy(bf16[1,128,512]{2,1,0:T(8,128)(2,1)} %bitcast.4) | data formatting | bytes 262144

commit v4 on v3

--- a/solution.py
+++ b/solution.py
@@ -119,9 +119,11 @@
     def q_arrived(t):
         remote(own_q, queries.at[t], q_send.at[0], q_recv.at[t], device(0, 0, 1 - core)).wait_recv()
 
-    def kv_arrived(t):
-        for j in range(2):
-            kv_remote(t, j).wait_recv()
+    def k_arrived(t):
+        kv_remote(t, 0).wait_recv()
+
+    def v_arrived(t):
+        kv_remote(t, 1).wait_recv()
 
     def kv_out(t):
         for j in range(2):
@@ -166,84 +168,6 @@
             remote(part_stats.at[t], got_stats.at[t], s_send.at[t], s_recv.at[t], target),
         ]
 
-    chunks = [slice(k, k + CHUNK) for k in range(0, KEYS, CHUNK)]
-    halves = [slice(0, W // 2), slice(W // 2, W)]
-
-    def tile(t, carry):
-        kv_arrived(t)
-
-        @pl.when(t == 0)
-        def _():
-            kv_out(2)
-            kv_out(3)
-
-        @pl.when(t == 1)
-        def _():
-            kv_out(4)
-            kv_out(5)
-
-        @pl.when(t == 2)
-        def _():
-            q_arrived(2)
-            q_copies[6].start()
-            kv_out(6)
-            kv_out(7)
-
-        @pl.when((t == 3) | (t == 4) | (t == 5) | (t == 7))
-        def _():
-            q_arrived(t)
-
-        q_rows = heads_in_rows(queries[t])
-
-        def score(n, at):
-            s = lax.dot_general(keys[t, at, :], q_rows[halves[n]], NT, preferred_element_type=F32)
-            scores[at, halves[n]] = s
-            return jnp.max(s, axis=0, keepdims=True)
-
-        def soften(n, peak, at):
-            probs[at, halves[n]] = jnp.exp2((scores[at, halves[n]] - peak) * SCALE).astype(BF16)
-
-        def finish(n, peak):
-            sums = jnp.dot(values_t[...], probs[:, halves[n]], preferred_element_type=F32)
-            parts[t, :, halves[n]] = sums[:HD].astype(BF16)
-            for k in range(HERE // 2):
-                at, head = slice(k * LS, (k + 1) * LS), n * HERE // 2 + k
-                part_stats[t, head : head + 1, :] = peak[:, at]
-                part_stats[t, HERE + head : HERE + head + 1, :] = sums[HD : HD + 1, at]
-
-        peak = functools.reduce(jnp.maximum, [score(0, at) for at in chunks])
-        values_t[:HD, :] = values[t].T
-        next_peak = []
-        for at in chunks:
-            next_peak.append(score(1, at))
-            soften(0, peak, at)
-        next_peak = functools.reduce(jnp.maximum, next_peak)
-
-        @pl.when(t == 0)
-        def _():
-            q_arrived(1)
-            q_copies[3].start()
-            q_copies[4].start()
-
-        finish(0, peak)
-        for at in chunks:
-            soften(1, next_peak, at)
-        finish(1, next_peak)
-
-        @pl.when((t != 0) & (t != 6))
-        def _():
-            for copy in out_copies(t):
-                copy.start()
-
-        @pl.when(t == 1)
-        def _():
-            q_arrived(6)
-            q_copies[5].start()
-
-        return carry
-
-    lax.fori_loop(0, TILES, tile, 0)
-
     def add(pieces, k):
         lanes = slice(k * LS, (k + 1) * LS)
         peaks = [at[k : k + 1, :] for _, at in pieces]
@@ -268,10 +192,89 @@
                 copy.wait_recv()
         return [(got.at[t], got_stats.at[t]) for t in ts]
 
-    near = parts.at[6], part_stats.at[6]
-    fold([near] + arrived((3, 4)), *near)
-    for copy in out_copies(6):
-        copy.start()
+    chunks = [slice(k, k + CHUNK) for k in range(0, KEYS, CHUNK)]
+    halves = [slice(0, W // 2), slice(W // 2, W)]
+
+    def tile(t, carry):
+        k_arrived(t)
+
+        @pl.when(t == 0)
+        def _():
+            kv_out(2)
+            kv_out(3)
+            q_arrived(1)
+            q_copies[3].start()
+            q_copies[4].start()
+
+        @pl.when(t == 1)
+        def _():
+            kv_out(4)
+            kv_out(5)
+
+        @pl.when(t == 2)
+        def _():
+            q_arrived(2)
+            q_copies[6].start()
+            kv_out(6)
+            kv_out(7)
+
+        @pl.when((t == 3) | (t == 4) | (t == 5) | (t == 7))
+        def _():
+            q_arrived(t)
+
+        q_rows = heads_in_rows(queries[t])
+
+        def score(n, at):
+            s = lax.dot_general(keys[t, at, :], q_rows[halves[n]], NT, preferred_element_type=F32)
+            scores[at, halves[n]] = s
+            return jnp.max(s, axis=0, keepdims=True)
+
+        def soften(n, peak, at):
+            probs[at, halves[n]] = jnp.exp2((scores[at, halves[n]] - peak) * SCALE).astype(BF16)
+
+        def finish(n, peak):
+            sums = jnp.dot(values_t[...], probs[:, halves[n]], preferred_element_type=F32)
+            parts[t, :, halves[n]] = sums[:HD].astype(BF16)
+            for k in range(HERE // 2):
+                at, head = slice(k * LS, (k + 1) * LS), n * HERE // 2 + k
+                part_stats[t, head : head + 1, :] = peak[:, at]
+                part_stats[t, HERE + head : HERE + head + 1, :] = sums[HD : HD + 1, at]
+
+        peak = functools.reduce(jnp.maximum, [score(0, at) for at in chunks])
+        v_arrived(t)
+        values_t[:HD, :] = values[t].T
+        next_peak = []
+        for at in chunks:
+            next_peak.append(score(1, at))
+            soften(0, peak, at)
+        next_peak = functools.reduce(jnp.maximum, next_peak)
+
+        @pl.when(t == 7)
+        def _():
+            near = parts.at[6], part_stats.at[6]
+            fold([near] + arrived((3, 4)), *near)
+            for copy in out_copies(6):
+                copy.start()
+
+        finish(0, peak)
+        for at in chunks:
+            soften(1, next_peak, at)
+        finish(1, next_peak)
+
+        @pl.when((t != 0) & (t != 6))
+        def _():
+            for copy in out_copies(t):
+                copy.start()
+
+        @pl.when(t == 0)
+        def _():
+            q_arrived(6)
+            q_copies[5].start()
+
+        return carry
+
+    lax.fori_loop(0, TILES, tile, 0)
+
     so_far = total, stats
     fold([so_far, (parts.at[0], part_stats.at[0])] + arrived((1, 2)), *so_far)
     pieces = [so_far] + arrived((7, 5, 6))

time: 37.9 us -> 36.2 us (0.955)
  the two profiles are of different devices: /device:TPU:22 before, /device:TPU:1 now
where the time goes in v4:
time: 36.2 us; the launch traced here: 35.9 us
  Pallas kernels  33.7 us (93%)
  local copies, waits for them, and re-layouts  1.57 us (4%)
  between operations  0.66 us (2%)
    pallas_call x1, Pallas kernels, on_device(): pl.pallas_call(kernel, name='attend', out_shape=jax.ShapeDtypeStruct((LS,...  33.7 us
    unnamed x1, local copies, waits for them, and re-layouts  1.57 us

profile of v4, /device:TPU:1, one launch (start us, length us, event | category | flops | bytes accessed | tf_op | source)
XLA Modules:
  0.0 35.9 jit_solution(13517434506536736456)
XLA Ops:
  0.7 33.7 %attend.1 = bf16[128,512]{1,0:T(8,128)(2,1)} custom-call(bf16[128,512]{1,0:T(8,128)(2,1)} %bitcast.7, bf16[128,1024]{1,0:T(8,128)(2,1)} %bitcast.5, bf16[128,1024]{1,0:T(8,128)(2,1)} %bitcast.6, bf16[1024,1024]{1,0:T(8,128)(2,1)} %pk_hbm.1, bf16[1024,1024]{1,0:T(8,128)(2,1)} %pv_hbm.1, s32[1]{0:T(128)S(6)} %copy.8.len_ref), custom_call_target="tpu_custom_call" | custom-call | flops 4294967296 | bytes 6291456 | tf_op jit(solution)/shard_map/attend/pallas_call | solution.py:300
  34.3 1.6 %copy.9 = bf16[1,128,512]{2,1,0:T(8,128)(2,1)} copy(bf16[1,128,512]{2,1,0:T(8,128)(2,1)} %bitcast.4) | data formatting | bytes 262144

commit v5 on v4

--- a/solution.py
+++ b/solution.py
@@ -23,7 +23,7 @@
 SIDE = (0, 0, 0, 1, 1, 1, 1, 0)
 SENT_TO = (0, 0, 0, 0, 0, 1, 1, 0)
 MIRROR = (0, 7, 2, 4, 3, 5, 6, 1)
-ONES = 8
+ONES = 16
 
 
 MESH = pl.DeviceIdType.MESH
@@ -277,7 +277,8 @@
 
     so_far = total, stats
     fold([so_far, (parts.at[0], part_stats.at[0])] + arrived((1, 2)), *so_far)
-    pieces = [so_far] + arrived((7, 5, 6))
+    fold([so_far] + arrived((7,)), *so_far)
+    pieces = [so_far] + arrived((5, 6))
     live = lax.broadcasted_iota(jnp.int32, (LS, HD), 0) < len_ref[0]
     for k in range(HERE):
         over, under, _ = add(pieces, k)

time: 36.2 us -> 36.2 us (level)
  no operation moved by 1% of the time
where the time goes in v5:
time: 36.2 us; the launch traced here: 35.9 us
  Pallas kernels  33.7 us (93%)
  local copies, waits for them, and re-layouts  1.57 us (4%)
  between operations  0.66 us (2%)
    pallas_call x1, Pallas kernels, on_device(): pl.pallas_call(kernel, name='attend', out_shape=jax.ShapeDtypeStruct((LS,...  33.7 us
    unnamed x1, local copies, waits for them, and re-layouts  1.57 us

profile of v5, /device:TPU:1, one launch (start us, length us, event | category | flops | bytes accessed | tf_op | source)
XLA Modules:
  0.0 35.9 jit_solution(17203895916747164491)
XLA Ops:
  0.7 33.7 %attend.1 = bf16[128,512]{1,0:T(8,128)(2,1)} custom-call(bf16[128,512]{1,0:T(8,128)(2,1)} %bitcast.7, bf16[128,1024]{1,0:T(8,128)(2,1)} %bitcast.5, bf16[128,1024]{1,0:T(8,128)(2,1)} %bitcast.6, bf16[1024,1024]{1,0:T(8,128)(2,1)} %pk_hbm.1, bf16[1024,1024]{1,0:T(8,128)(2,1)} %pv_hbm.1, s32[1]{0:T(128)S(6)} %copy.8.len_ref), custom_call_target="tpu_custom_call" | custom-call | flops 4294967296 | bytes 6291456 | tf_op jit(solution)/shard_map/attend/pallas_call | solution.py:301
  34.4 1.6 %copy.9 = bf16[1,128,512]{2,1,0:T(8,128)(2,1)} copy(bf16[1,128,512]{2,1,0:T(8,128)(2,1)} %bitcast.4) | data formatting | bytes 262144
